TPU v7x, 256 devices: a whole 4x4x8 slice. The times are simulated.
256 devices in a mesh: in: 4 (over y_hi, core), out: 8 (over y_lo, x), depth: 8 (over z).
Axes of the slice: x: 4, y: 4 (y_hi: 2, y_lo: 2; y = y_hi * 2 + y_lo), z: 8, core: 2. Of those that a mesh axis runs over, the one named last changes fastest.
Arguments:
- inputs: bfloat16 [4096, 6144], P(('depth', 'out'), 'in'), may hold values from -6 to 6
- weight: bfloat16 [6144, 24576], P(('in', 'depth'), 'out'), may hold values from -0.078125 to 0.078125
- cotangent: bfloat16 [4096, 24576], P(('depth', 'in'), 'out'), may hold values from -6 to 6
Outputs:
- activated: bfloat16 [4096, 24576], P(('depth', 'in'), 'out')
- grad_inputs: bfloat16 [4096, 6144], P(('depth', 'out'), 'in')
- grad_weight: bfloat16 [6144, 24576], P(('in', 'depth'), 'out')
All inputs are finite; a program needn't handle non-finite values.
Results may differ from a plain program's by a relative error of at most 0.005.
Values may be sent and summed in bfloat16 or wider, within the bound.
No kernel may reach another device: no remote copies, remote signals or barrier semaphores. Data moves between devices by JAX's collectives and lax.ppermute only.
A program may use at most 128 MiB of HBM per device.

v0:
```python
import math

import jax
import jax.numpy as jnp
from jax import lax
from jax.sharding import PartitionSpec as P

slope_c = math.sqrt(2.0 / math.pi)
WIDTHS = (1536, 1536)
bf16 = jnp.bfloat16


def gelu_both(value):
    inner = slope_c * (value + 0.044715 * value * value * value)
    t = jnp.tanh(inner)
    act = 0.5 * value * (1.0 + t)
    slope = 0.5 * (1.0 + t) + 0.5 * value * (1.0 - t * t) * slope_c * (
        1.0 + 3.0 * 0.044715 * value * value
    )
    return act, slope


def mm(a, b):
    return jnp.dot(a, b, preferred_element_type=jnp.float32)


def tie(value, *earlier):
    return lax.optimization_barrier((value, *earlier))[0] if earlier else value


def body(inputs, weight, cotangent):
    nz = lax.axis_size("depth")
    z = lax.axis_index("depth")
    i = lax.axis_index("in")
    up = [(s, (s + 1) % nz) for s in range(nz)]
    down = [(s, (s - 1) % nz) for s in range(nz)]
    core = [(s, s ^ 1) for s in range(4)]
    yhi = [(s, s ^ 2) for s in range(4)]

    def send(value, axis, pairs, name):
        with jax.named_scope(name):
            return lax.ppermute(value, axis, pairs)

    wr = weight.shape[0]
    half = wr // 2
    rows = cotangent.shape[0]
    cols = [slice(0, WIDTHS[0]), slice(WIDTHS[0], WIDTHS[0] + WIDTHS[1])]

    o = lax.axis_index("out")
    nx = 4
    right = [(s, s // nx * nx + (s + 1) % nx) for s in range(2 * nx)]
    left = [(s, s // nx * nx + (s - 1) % nx) for s in range(2 * nx)]
    ylo = [(s, (s + nx) % (2 * nx)) for s in range(2 * nx)]

    def at(k):
        return lax.rem(z + k, nz)

    def token_block(dx, other):
        mate = lax.rem(o // nx + other, 2) * nx + lax.rem(lax.rem(o, nx) + nx + dx, nx)
        k = i ^ (mate // 2)
        return 2 * (2 * (k % 2) + k // 2) + mate % 2

    def sum_out(g):
        g = g.reshape(2 * nx, inputs.shape[0], -1)

        def block(dx, other):
            return lax.dynamic_index_in_dim(g, token_block(dx, other), 0, keepdims=False)

        u = send(block(2, 0).astype(bf16), "out", right, "g_r1")
        d = send(block(-2, 1).astype(bf16), "out", left, "g_l1")
        u = jnp.stack([block(1, 0) + u, block(1, 1)]).astype(bf16)
        d = jnp.stack([block(-1, 0), block(-1, 1) + d]).astype(bf16)
        u, d = send(u, "out", right, "g_r2"), send(d, "out", left, "g_l2")
        own = block(0, 0) + u[0] + d[0]
        other = block(0, 1) + u[1] + d[1]
        return own + send(other.astype(bf16), "out", ylo, "g_ylo")

    def gather(own):
        w = lax.dynamic_update_index_in_dim(jnp.zeros((nz, wr, own.shape[1]), bf16), own, z, 0)
        u = d = own
        got = []
        for hop in range(1, 5):
            if hop == 4:
                u, d = u[:half], d[half:]
            u = send(u, "depth", up, f"gather_u{hop}")
            d = send(d, "depth", down, f"gather_d{hop}")
            w = lax.dynamic_update_slice(w, u[None], (at(nz - hop), 0, 0))
            w = lax.dynamic_update_slice(w, d[None], (at(hop), half if hop == 4 else 0, 0))
            got.append(u)
        return w.reshape(nz * wr, -1), got

    def sum_in(pre, name):
        both = pre[: 2 * rows] + send(pre[2 * rows :], "in", core, f"{name}_core")
        return both, lambda: both[:rows] + send(both[rows:].astype(bf16), "in", yhi, f"{name}_yhi")

    def hidden(pre, ct):
        act, slope = gelu_both(pre)
        return act.astype(bf16), (ct.astype(jnp.float32) * slope).astype(bf16)

    def gather_in(dh, name):
        dh = jnp.concatenate([dh, send(dh, "in", yhi, f"{name}_yhi")], axis=0)
        return jnp.concatenate([dh, send(dh, "in", core, f"{name}_core")], axis=0)

    def back(dh, w):
        return lax.dot_general(dh, w, (((1,), (1,)), ((), ())), preferred_element_type=jnp.float32)

    def sum_z(dh, name, beside):
        far = mm(lax.dynamic_index_in_dim(xt.reshape(nz, wr, -1), at(4), 0, keepdims=False), dh).astype(bf16)
        u = send(far[:half], "depth", up, f"{name}_u1")
        d = send(far[half:], "depth", down, f"{name}_d1")
        parts = mm(xt, tie(dh, far)).reshape(nz, wr, -1)
        work = beside(far)

        def part(k, lo=0, n=wr):
            return lax.dynamic_slice(parts, (at(k), lo, 0), (1, n, parts.shape[2]))[0]

        for hop in range(2, 5):
            if hop == 2:
                u = jnp.concatenate([part(3, 0, half) + u, part(3, half, half)], axis=0)
                d = jnp.concatenate([part(5, 0, half), part(5, half, half) + d], axis=0)
            else:
                u, d = part(5 - hop) + u, part(3 + hop) + d
            u, d = u.astype(bf16), d.astype(bf16)
            u, d = tie(u, d, *work[hop - 2]), tie(d, u, *work[hop - 2])
            u = send(u, "depth", up, f"{name}_u{hop}")
            d = send(d, "depth", down, f"{name}_d{hop}")
        return (part(0) + u + d).astype(bf16), work

    x_group = lax.all_gather(inputs, "out", axis=0, tiled=True)
    w0, got = gather(weight[:, cols[0]])
    blocks = [lax.dynamic_slice_in_dim(x_group, (i ^ k) * rows, rows, axis=0) for k in (0, 2, 1, 3)]
    x = jnp.concatenate(blocks, axis=0)
    xt = lax.optimization_barrier(x.T)
    w1 = lax.all_gather(tie(weight[:, cols[1]], got[1]), "depth", axis=0, tiled=True)

    _, rest = sum_in(mm(x, w0), "pre0")
    act0, dh0 = hidden(rest(), cotangent[:, cols[0]])
    dh0 = gather_in(dh0, "dh0")
    p0 = mm(xt, dh0).astype(bf16)
    gw0 = lax.psum_scatter(p0, "depth", scatter_dimension=0, tiled=True)

    both, rest = sum_in(mm(tie(x, p0), w1), "pre1")
    gi = back(tie(dh0, both), w0)
    act1, dh1 = hidden(rest(), cotangent[:, cols[1]])
    dh1 = gather_in(tie(dh1, gi), "dh1")
    ring = 1024

    def beside(far):
        g = gi + back(tie(dh1, far), w1)
        p2 = mm(xt, tie(dh1[:, ring:], far)).astype(bf16)
        return (g,), (p2, gw0), ()

    gw1, ((g,), (p2, _), _) = sum_z(dh1[:, :ring], "sum1", beside)
    gw2 = lax.psum_scatter(p2, "depth", scatter_dimension=0, tiled=True)
    g = sum_out(g)
    return (
        jnp.concatenate([act0, act1], axis=1),
        g.astype(bf16),
        jnp.concatenate([gw0, gw1, gw2], axis=1),
    )


def solution(mesh):
    in_specs = (P(("depth", "out"), "in"), P(("in", "depth"), "out"), P(("depth", "in"), "out"))
    out_specs = (P(("depth", "in"), "out"), P(("depth", "out"), "in"), P(("in", "depth"), "out"))
    return jax.shard_map(body, mesh=mesh, in_specs=in_specs, out_specs=out_specs, check_vma=False)
```

profile of v0, /device:TPU:1, one launch (start us, length us, event | category | flops | bytes accessed | tf_op | source)
XLA Modules:
  0.0 236.8 jit_solution(13536038444661549760)
XLA Ops:
  12.5 3.9 %collective-permute-start.1 = (bf16[192,1536]{1,0:T(8,128)(2,1)S(1)}, bf16[192,1536]{1,0:T(8,128)(2,1)S(1)}, u32[]{:S(2)}, u32[]{:S(2)}) collective-permute-start(bf16[192,1536]{1,0:T(8,128)(2,1)S(1)} %get-tuple-element.54), channel_id=1, source_target_pairs={{0,7},{1,0},{2,1},{3,2},{4,3},{5,4},{6,5},{7,6},{8,15},{9,8},{10,9... | collective-permute-start | bytes 1769480 | tf_op jit(solution)/shard_map/gather_d1/ppermute | solution.py:42
  16.5 2.5 %broadcast_in_dim.31 = bf16[8,192,1536]{2,1,0:T(8,128)(2,1)} broadcast(bf16[]{:T(256)} %constant.303.clone.1), dimensions={} | broadcast | bytes 4718594 | tf_op jit(solution)/shard_map/broadcast_in_dim | solution.py:79
  19.9 9.8 %collective-permute-done = bf16[192,1536]{1,0:T(8,128)(2,1)S(1)} collective-permute-done((bf16[192,1536]{1,0:T(8,128)(2,1)S(1)}, bf16[192,1536]{1,0:T(8,128)(2,1)S(1)}, u32[]{:S(2)}, u32[]{:S(2)}) %collective-permute-start) | collective-permute-done | bytes 589856 | tf_op jit(solution)/shard_map/gather_u1/ppermute | solution.py:42
  29.6 2.7 %collective-permute-start.3 = (bf16[192,1536]{1,0:T(8,128)(2,1)S(1)}, bf16[192,1536]{1,0:T(8,128)(2,1)S(1)}, u32[]{:S(2)}, u32[]{:S(2)}) collective-permute-start(bf16[192,1536]{1,0:T(8,128)(2,1)S(1)} %collective-permute-done.1), channel_id=1, source_target_pairs={{0,7},{1,0},{2,1},{3,2},{4,3},{5,4},{6,5},{7,6},{8,15},{9,8},{10,9... | collective-permute-start | bytes 1769480 | tf_op jit(solution)/shard_map/gather_d2/ppermute | solution.py:42
  34.1 10.5 %collective-permute-done.2 = bf16[192,1536]{1,0:T(8,128)(2,1)S(1)} collective-permute-done((bf16[192,1536]{1,0:T(8,128)(2,1)S(1)}, bf16[192,1536]{1,0:T(8,128)(2,1)S(1)}, u32[]{:S(2)}, u32[]{:S(2)}) %collective-permute-start.2) | collective-permute-done | bytes 589856 | tf_op jit(solution)/shard_map/gather_u2/ppermute | solution.py:42
  44.7 2.7 %collective-permute-start.5 = (bf16[192,1536]{1,0:T(8,128)(2,1)S(1)}, bf16[192,1536]{1,0:T(8,128)(2,1)S(1)}, u32[]{:S(2)}, u32[]{:S(2)}) collective-permute-start(bf16[192,1536]{1,0:T(8,128)(2,1)S(1)} %collective-permute-done.3), channel_id=1, source_target_pairs={{0,7},{1,0},{2,1},{3,2},{4,3},{5,4},{6,5},{7,6},{8,15},{9,8},{10,9... | collective-permute-start | bytes 1769480 | tf_op jit(solution)/shard_map/gather_d3/ppermute | solution.py:42
  49.1 9.5 %collective-permute-done.4 = bf16[192,1536]{1,0:T(8,128)(2,1)S(1)} collective-permute-done((bf16[192,1536]{1,0:T(8,128)(2,1)S(1)}, bf16[192,1536]{1,0:T(8,128)(2,1)S(1)}, u32[]{:S(2)}, u32[]{:S(2)}) %collective-permute-start.4) | collective-permute-done | bytes 589856 | tf_op jit(solution)/shard_map/gather_u3/ppermute | solution.py:42
  58.8 2.7 %collective-permute-start.7 = (bf16[96,1536]{1,0:T(8,128)(2,1)S(1)}, bf16[96,1536]{1,0:T(8,128)(2,1)S(1)}, u32[]{:S(2)}, u32[]{:S(2)}) collective-permute-start(bf16[96,1536]{1,0:T(8,128)(2,1)S(1)} %slice.91), channel_id=1, source_target_pairs={{0,7},{1,0},{2,1},{3,2},{4,3},{5,4},{6,5},{7,6},{8,15},{9,8},{10,9... | collective-permute-start | bytes 884744 | tf_op jit(solution)/shard_map/gather_d4/ppermute | solution.py:42
  69.4 4.7 %fusion.37 = f32[512,1536]{1,0:T(8,128)S(1)} fusion(bf16[1536,1536]{1,0:T(8,128)(2,1)} %bitcast.9, bf16[128,1536]{0,1:T(8,128)(2,1)S(1)} %copy.14, bf16[128,1536]{0,1:T(8,128)(2,1)S(1)} %copy.13, bf16[128,1536]{0,1:T(8,128)(2,1)S(1)} %copy.12, bf16[128,1536]{0,1:T(8,128)(2,1)S(1)} %copy.11), kind=kOutput, calls=%fused_computation.96 | convolution fusion | flops 2422210560 | bytes 9437184 | tf_op jit(solution)/shard_map/dot_general | solution.py:24
  74.2 4.1 %collective-permute-start.8 = (f32[256,1536]{1,0:T(8,128)S(1)}, f32[256,1536]{1,0:T(8,128)S(1)}, u32[]{:S(2)}, u32[]{:S(2)}) collective-permute-start(f32[256,1536]{1,0:T(8,128)S(1)} %slice.93), channel_id=1, source_target_pairs={{0,64},{64,0},{128,192},{192,128},{1,65},{65,1},{129,193},{193,129... | collective-permute-start | bytes 4718600 | tf_op jit(solution)/shard_map/pre0_core/ppermute | solution.py:42
  78.4 3.0 %collective-permute-done.8 = f32[256,1536]{1,0:T(8,128)S(1)} collective-permute-done((f32[256,1536]{1,0:T(8,128)S(1)}, f32[256,1536]{1,0:T(8,128)S(1)}, u32[]{:S(2)}, u32[]{:S(2)}) %collective-permute-start.8) | collective-permute-done | bytes 1572896 | tf_op jit(solution)/shard_map/pre0_core/ppermute | solution.py:42
  81.7 3.1 %collective-permute-start.9 = (bf16[128,1536]{1,0:T(8,128)(2,1)S(1)}, bf16[128,1536]{1,0:T(8,128)(2,1)S(1)}, u32[]{:S(2)}, u32[]{:S(2)}) collective-permute-start(bf16[128,1536]{1,0:T(8,128)(2,1)S(1)} %slice.132), channel_id=1, source_target_pairs={{0,128},{64,192},{128,0},{192,64},{1,129},{65,193},{129,1},{193,65... | collective-permute-start | bytes 1179656 | tf_op jit(solution)/shard_map/pre0_yhi/ppermute | solution.py:42
  84.8 8.9 %collective-permute-done.9 = bf16[128,1536]{1,0:T(8,128)(2,1)S(1)} collective-permute-done((bf16[128,1536]{1,0:T(8,128)(2,1)S(1)}, bf16[128,1536]{1,0:T(8,128)(2,1)S(1)}, u32[]{:S(2)}, u32[]{:S(2)}) %collective-permute-start.9) | collective-permute-done | bytes 393248 | tf_op jit(solution)/shard_map/pre0_yhi/ppermute | solution.py:42
  94.4 3.1 %collective-permute-start.10 = (bf16[128,1536]{1,0:T(8,128)(2,1)S(1)}, bf16[128,1536]{1,0:T(8,128)(2,1)S(1)}, u32[]{:S(2)}, u32[]{:S(2)}) collective-permute-start(bf16[128,1536]{1,0:T(8,128)(2,1)S(1)} %get-tuple-element.46), channel_id=1, source_target_pairs={{0,128},{64,192},{128,0},{192,64},{1,129},{65,193},{129,1},{193,65... | collective-permute-start | bytes 1179656 | tf_op jit(solution)/shard_map/dh0_yhi/ppermute | solution.py:42
  97.5 8.1 %collective-permute-done.10 = bf16[128,1536]{1,0:T(8,128)(2,1)S(1)} collective-permute-done((bf16[128,1536]{1,0:T(8,128)(2,1)S(1)}, bf16[128,1536]{1,0:T(8,128)(2,1)S(1)}, u32[]{:S(2)}, u32[]{:S(2)}) %collective-permute-start.10) | collective-permute-done | bytes 393248 | tf_op jit(solution)/shard_map/dh0_yhi/ppermute | solution.py:42
  111.3 4.3 %convolution_convert_fusion = bf16[1536,1536]{1,0:T(8,128)(2,1)} fusion(bf16[1536,512]{1,0:T(8,128)(2,1)S(1)} %get-tuple-element.47, bf16[256,1536]{1,0:T(8,128)(2,1)S(1)} %collective-permute-done.11, bf16[128,1536]{1,0:T(8,128)(2,1)S(1)} %collective-permute-done.10, bf16[128,1536]{1,0:T(8,128)(2,1)S(1)} %get-tuple-element.46), kind=kOutput, calls=%fused_computation | convolution fusion | flops 2422996992 | bytes 7864320 | tf_op jit(solution)/shard_map/dot_general | solution.py:24
  118.1 4.6 %fusion.40 = f32[512,1536]{1,0:T(8,128)S(1)} fusion(bf16[512,1536]{0,1:T(8,128)(2,1)S(1)} %copy-done.4, bf16[1536,1536]{1,0:T(8,128)(2,1)} %all-gather.5.cloned.1.call-done), kind=kOutput, calls=%fused_computation.99 | convolution fusion | flops 2415919104 | bytes 9437184 | tf_op jit(solution)/shard_map/dot_general | solution.py:24
  123.9 2.7 %collective-permute-done.12 = f32[256,1536]{1,0:T(8,128)S(1)} collective-permute-done((f32[256,1536]{1,0:T(8,128)S(1)}, f32[256,1536]{1,0:T(8,128)S(1)}, u32[]{:S(2)}, u32[]{:S(2)}) %collective-permute-start.12) | collective-permute-done | bytes 1572896 | tf_op jit(solution)/shard_map/pre1_core/ppermute | solution.py:42
  126.9 2.8 %collective-permute-start.13 = (bf16[128,1536]{1,0:T(8,128)(2,1)S(1)}, bf16[128,1536]{1,0:T(8,128)(2,1)S(1)}, u32[]{:S(2)}, u32[]{:S(2)}) collective-permute-start(bf16[128,1536]{1,0:T(8,128)(2,1)S(1)} %slice.131), channel_id=1, source_target_pairs={{0,128},{64,192},{128,0},{192,64},{1,129},{65,193},{129,1},{193,65... | collective-permute-start | bytes 1179656 | tf_op jit(solution)/shard_map/pre1_yhi/ppermute | solution.py:42
  129.7 7.1 %fusion.41 = f32[512,1536]{1,0:T(8,128)} fusion(bf16[512,1536]{1,0:T(8,128)(2,1)S(1)} %pad_maximum_fusion.1, bf16[1536,1536]{1,0:T(8,128)(2,1)} %bitcast.9), kind=kOutput, calls=%fused_computation.100 | convolution fusion | flops 2415919104 | bytes 9437184 | tf_op jit(solution)/shard_map/dot_general | solution.py:105
  140.1 2.8 %collective-permute-start.14 = (bf16[128,1536]{1,0:T(8,128)(2,1)S(1)}, bf16[128,1536]{1,0:T(8,128)(2,1)S(1)}, u32[]{:S(2)}, u32[]{:S(2)}) collective-permute-start(bf16[128,1536]{1,0:T(8,128)(2,1)S(1)} %get-tuple-element.19), channel_id=1, source_target_pairs={{0,128},{64,192},{128,0},{192,64},{1,129},{65,193},{129,1},{193,65... | collective-permute-start | bytes 1179656 | tf_op jit(solution)/shard_map/dh1_yhi/ppermute | solution.py:42
  143.0 8.1 %collective-permute-done.14 = bf16[128,1536]{1,0:T(8,128)(2,1)S(1)} collective-permute-done((bf16[128,1536]{1,0:T(8,128)(2,1)S(1)}, bf16[128,1536]{1,0:T(8,128)(2,1)S(1)}, u32[]{:S(2)}, u32[]{:S(2)}) %collective-permute-start.14) | collective-permute-done | bytes 393248 | tf_op jit(solution)/shard_map/dh1_yhi/ppermute | solution.py:42
  156.7 2.7 %collective-permute-start.22 = (bf16[96,1024]{1,0:T(8,128)(2,1)}, bf16[96,1024]{1,0:T(8,128)(2,1)}, u32[]{:S(2)}, u32[]{:S(2)}) collective-permute-start(bf16[96,1024]{1,0:T(8,128)(2,1)} %get-tuple-element.56), channel_id=1, source_target_pairs={{0,7},{1,0},{2,1},{3,2},{4,3},{5,4},{6,5},{7,6},{8,15},{9,8},{10,9... | collective-permute-start | bytes 589832 | tf_op jit(solution)/shard_map/sum1_d1/ppermute | solution.py:42
  159.3 4.5 %convolution_add_fusion = f32[512,1536]{1,0:T(8,128)S(1)} fusion(f32[512,1536]{1,0:T(8,128)S(1)} %copy-done.10, bf16[512,1536]{1,0:T(8,128)(2,1)S(1)} %constant_dynamic-update-slice_fusion, bf16[1536,1536]{1,0:T(8,128)(2,1)} %all-gather.5.cloned.1.call-done), kind=kOutput, calls=%fused_computation.1 | convolution fusion | flops 2416705536 | bytes 12582912 | tf_op jit(solution)/shard_map/dot_general | solution.py:105
  167.5 4.5 %fusion.42 = f32[1536,1024]{1,0:T(8,128)} fusion(bf16[1536,512]{1,0:T(8,128)(2,1)S(1)} %copy-done.3, bf16[512,1024]{1,0:T(8,128)(2,1)S(1)} %slice.100), kind=kOutput, calls=%fused_computation.101 | convolution fusion | flops 1610612736 | bytes 8912896 | tf_op jit(solution)/shard_map/dot_general | solution.py:24
  180.1 2.7 %collective-permute-start.24 = (bf16[192,1024]{1,0:T(8,128)(2,1)S(1)}, bf16[192,1024]{1,0:T(8,128)(2,1)S(1)}, u32[]{:S(2)}, u32[]{:S(2)}) collective-permute-start(bf16[192,1024]{1,0:T(8,128)(2,1)S(1)} %get-tuple-element.23), channel_id=1, source_target_pairs={{0,7},{1,0},{2,1},{3,2},{4,3},{5,4},{6,5},{7,6},{8,15},{9,8},{10,9... | collective-permute-start | bytes 1179656 | tf_op jit(solution)/shard_map/sum1_d2/ppermute | solution.py:42
  184.8 5.4 %collective-permute-done.23 = bf16[192,1024]{1,0:T(8,128)(2,1)S(1)} collective-permute-done((bf16[192,1024]{1,0:T(8,128)(2,1)S(1)}, bf16[192,1024]{1,0:T(8,128)(2,1)S(1)}, u32[]{:S(2)}, u32[]{:S(2)}) %collective-permute-start.23) | collective-permute-done | bytes 393248 | tf_op jit(solution)/shard_map/sum1_u2/ppermute | solution.py:42
  192.6 2.7 %collective-permute-start.26 = (bf16[192,1024]{1,0:T(8,128)(2,1)S(1)}, bf16[192,1024]{1,0:T(8,128)(2,1)S(1)}, u32[]{:S(2)}, u32[]{:S(2)}) collective-permute-start(bf16[192,1024]{1,0:T(8,128)(2,1)S(1)} %get-tuple-element.26), channel_id=1, source_target_pairs={{0,7},{1,0},{2,1},{3,2},{4,3},{5,4},{6,5},{7,6},{8,15},{9,8},{10,9... | collective-permute-start | bytes 1179656 | tf_op jit(solution)/shard_map/sum1_d3/ppermute | solution.py:42
  197.7 4.2 %collective-permute-done.25 = bf16[192,1024]{1,0:T(8,128)(2,1)S(1)} collective-permute-done((bf16[192,1024]{1,0:T(8,128)(2,1)}, bf16[192,1024]{1,0:T(8,128)(2,1)S(1)}, u32[]{:S(2)}, u32[]{:S(2)}) %collective-permute-start.25) | collective-permute-done | bytes 393248 | tf_op jit(solution)/shard_map/sum1_u3/ppermute | solution.py:42
  205.0 3.5 %collective-permute-start.28 = (bf16[192,1024]{1,0:T(8,128)(2,1)S(1)}, bf16[192,1024]{1,0:T(8,128)(2,1)S(1)}, u32[]{:S(2)}, u32[]{:S(2)}) collective-permute-start(bf16[192,1024]{1,0:T(8,128)(2,1)S(1)} %get-tuple-element.28), channel_id=1, source_target_pairs={{0,7},{1,0},{2,1},{3,2},{4,3},{5,4},{6,5},{7,6},{8,15},{9,8},{10,9... | collective-permute-start | bytes 1179656 | tf_op jit(solution)/shard_map/sum1_d4/ppermute | solution.py:42
  210.3 10.5 %collective-permute-done.28 = bf16[192,1024]{1,0:T(8,128)(2,1)S(1)} collective-permute-done((bf16[192,1024]{1,0:T(8,128)(2,1)S(1)}, bf16[192,1024]{1,0:T(8,128)(2,1)S(1)}, u32[]{:S(2)}, u32[]{:S(2)}) %collective-permute-start.28) | collective-permute-done | bytes 393248 | tf_op jit(solution)/shard_map/sum1_d4/ppermute | solution.py:42
  223.9 4.1 %reduce-scatter.5.cloned.1.call-done = bf16[192,512]{1,0:T(8,128)(2,1)} async-done(((bf16[1536,512]{1,0:T(8,128)(2,1)}), bf16[192,512]{1,0:T(8,128)(2,1)}) %reduce-scatter.5.cloned.1.call-update) | async-done | bytes 196624 | tf_op jit(solution)/shard_map/reduce_scatter | solution.py:154
  (118 shorter events, 66.4 us)
Async XLA Ops:
  7.2 59.9 %all-gather.3.cloned.1.call-start = ((), (), s32[]{:S(2)}) async-start(), calls=%async_computation.2 | async-start | bytes 1769472 | tf_op jit(solution)/shard_map/all_gather | solution.py:129
  7.9 110.2 %all-gather.5.cloned.1.call-start = ((), (), s32[]{:S(2)}) async-start(), calls=%async_computation.3 | async-start | bytes 5308416 | tf_op jit(solution)/shard_map/all_gather | solution.py:134
  10.1 19.6 %collective-permute-start = (bf16[192,1536]{1,0:T(8,128)(2,1)S(1)}, bf16[192,1536]{1,0:T(8,128)(2,1)S(1)}, u32[]{:S(2)}, u32[]{:S(2)}) collective-permute-start(bf16[192,1536]{1,0:T(8,128)(2,1)S(1)} %get-tuple-element.54), channel_id=1, source_target_pairs={{0,1},{1,2},{2,3},{3,4},{4,5},{5,6},{6,7},{7,0},{8,9},{9,10},{10,1... | collective-permute-start | bytes 1769480 | tf_op jit(solution)/shard_map/gather_u1/ppermute | solution.py:42
  12.5 17.1 %collective-permute-start.1 = (bf16[192,1536]{1,0:T(8,128)(2,1)S(1)}, bf16[192,1536]{1,0:T(8,128)(2,1)S(1)}, u32[]{:S(2)}, u32[]{:S(2)}) collective-permute-start(bf16[192,1536]{1,0:T(8,128)(2,1)S(1)} %get-tuple-element.54), channel_id=1, source_target_pairs={{0,7},{1,0},{2,1},{3,2},{4,3},{5,4},{6,5},{7,6},{8,15},{9,8},{10,9... | collective-permute-start | bytes 1769480 | tf_op jit(solution)/shard_map/gather_d1/ppermute | solution.py:42
  29.6 14.9 %collective-permute-start.2 = (bf16[192,1536]{1,0:T(8,128)(2,1)S(1)}, bf16[192,1536]{1,0:T(8,128)(2,1)S(1)}, u32[]{:S(2)}, u32[]{:S(2)}) collective-permute-start(bf16[192,1536]{1,0:T(8,128)(2,1)S(1)} %collective-permute-done), channel_id=1, source_target_pairs={{0,1},{1,2},{2,3},{3,4},{4,5},{5,6},{6,7},{7,0},{8,9},{9,10},{10,1... | collective-permute-start | bytes 1769480 | tf_op jit(solution)/shard_map/gather_u2/ppermute | solution.py:42
  29.6 15.1 %collective-permute-start.3 = (bf16[192,1536]{1,0:T(8,128)(2,1)S(1)}, bf16[192,1536]{1,0:T(8,128)(2,1)S(1)}, u32[]{:S(2)}, u32[]{:S(2)}) collective-permute-start(bf16[192,1536]{1,0:T(8,128)(2,1)S(1)} %collective-permute-done.1), channel_id=1, source_target_pairs={{0,7},{1,0},{2,1},{3,2},{4,3},{5,4},{6,5},{7,6},{8,15},{9,8},{10,9... | collective-permute-start | bytes 1769480 | tf_op jit(solution)/shard_map/gather_d2/ppermute | solution.py:42
  44.6 148.0 %reduce-scatter.3.cloned.1.call-start = ((), (), s32[]{:S(2)}) async-start(), calls=%async_computation.4 | async-start | bytes 5308416 | tf_op jit(solution)/shard_map/reduce_scatter | solution.py:140
  44.6 14.1 %collective-permute-start.4 = (bf16[192,1536]{1,0:T(8,128)(2,1)S(1)}, bf16[192,1536]{1,0:T(8,128)(2,1)S(1)}, u32[]{:S(2)}, u32[]{:S(2)}) collective-permute-start(bf16[192,1536]{1,0:T(8,128)(2,1)S(1)} %collective-permute-done.2), channel_id=1, source_target_pairs={{0,1},{1,2},{2,3},{3,4},{4,5},{5,6},{6,7},{7,0},{8,9},{9,10},{10,1... | collective-permute-start | bytes 1769480 | tf_op jit(solution)/shard_map/gather_u3/ppermute | solution.py:42
  44.7 14.1 %collective-permute-start.5 = (bf16[192,1536]{1,0:T(8,128)(2,1)S(1)}, bf16[192,1536]{1,0:T(8,128)(2,1)S(1)}, u32[]{:S(2)}, u32[]{:S(2)}) collective-permute-start(bf16[192,1536]{1,0:T(8,128)(2,1)S(1)} %collective-permute-done.3), channel_id=1, source_target_pairs={{0,7},{1,0},{2,1},{3,2},{4,3},{5,4},{6,5},{7,6},{8,15},{9,8},{10,9... | collective-permute-start | bytes 1769480 | tf_op jit(solution)/shard_map/gather_d3/ppermute | solution.py:42
  58.7 6.9 %collective-permute-start.6 = (bf16[96,1536]{1,0:T(8,128)(2,1)S(1)}, bf16[96,1536]{1,0:T(8,128)(2,1)S(1)}, u32[]{:S(2)}, u32[]{:S(2)}) collective-permute-start(bf16[96,1536]{1,0:T(8,128)(2,1)S(1)} %slice.90), channel_id=1, source_target_pairs={{0,1},{1,2},{2,3},{3,4},{4,5},{5,6},{6,7},{7,0},{8,9},{9,10},{10,1... | collective-permute-start | bytes 884744 | tf_op jit(solution)/shard_map/gather_u4/ppermute | solution.py:42
  58.8 7.5 %collective-permute-start.7 = (bf16[96,1536]{1,0:T(8,128)(2,1)S(1)}, bf16[96,1536]{1,0:T(8,128)(2,1)S(1)}, u32[]{:S(2)}, u32[]{:S(2)}) collective-permute-start(bf16[96,1536]{1,0:T(8,128)(2,1)S(1)} %slice.91), channel_id=1, source_target_pairs={{0,7},{1,0},{2,1},{3,2},{4,3},{5,4},{6,5},{7,6},{8,15},{9,8},{10,9... | collective-permute-start | bytes 884744 | tf_op jit(solution)/shard_map/gather_d4/ppermute | solution.py:42
  74.2 7.2 %collective-permute-start.8 = (f32[256,1536]{1,0:T(8,128)S(1)}, f32[256,1536]{1,0:T(8,128)S(1)}, u32[]{:S(2)}, u32[]{:S(2)}) collective-permute-start(f32[256,1536]{1,0:T(8,128)S(1)} %slice.93), channel_id=1, source_target_pairs={{0,64},{64,0},{128,192},{192,128},{1,65},{65,1},{129,193},{193,129... | collective-permute-start | bytes 4718600 | tf_op jit(solution)/shard_map/pre0_core/ppermute | solution.py:42
  81.7 12.0 %collective-permute-start.9 = (bf16[128,1536]{1,0:T(8,128)(2,1)S(1)}, bf16[128,1536]{1,0:T(8,128)(2,1)S(1)}, u32[]{:S(2)}, u32[]{:S(2)}) collective-permute-start(bf16[128,1536]{1,0:T(8,128)(2,1)S(1)} %slice.132), channel_id=1, source_target_pairs={{0,128},{64,192},{128,0},{192,64},{1,129},{65,193},{129,1},{193,65... | collective-permute-start | bytes 1179656 | tf_op jit(solution)/shard_map/pre0_yhi/ppermute | solution.py:42
  94.4 11.2 %collective-permute-start.10 = (bf16[128,1536]{1,0:T(8,128)(2,1)S(1)}, bf16[128,1536]{1,0:T(8,128)(2,1)S(1)}, u32[]{:S(2)}, u32[]{:S(2)}) collective-permute-start(bf16[128,1536]{1,0:T(8,128)(2,1)S(1)} %get-tuple-element.46), channel_id=1, source_target_pairs={{0,128},{64,192},{128,0},{192,64},{1,129},{65,193},{129,1},{193,65... | collective-permute-start | bytes 1179656 | tf_op jit(solution)/shard_map/dh0_yhi/ppermute | solution.py:42
  105.6 4.2 %collective-permute-start.11 = (bf16[256,1536]{1,0:T(8,128)(2,1)S(1)}, bf16[256,1536]{1,0:T(8,128)(2,1)S(1)}, u32[]{:S(2)}, u32[]{:S(2)}) collective-permute-start(bf16[256,1536]{1,0:T(8,128)(2,1)S(1)} %pad_maximum_fusion.3), channel_id=1, source_target_pairs={{0,64},{64,0},{128,192},{192,128},{1,65},{65,1},{129,193},{193,129... | collective-permute-start | bytes 2359304 | tf_op jit(solution)/shard_map/dh0_core/ppermute | solution.py:42
  115.6 112.4 %reduce-scatter.5.cloned.1.call-start = ((), (), s32[]{:S(2)}) async-start(), calls=%async_computation.5 | async-start | bytes 1769472 | tf_op jit(solution)/shard_map/reduce_scatter | solution.py:154
  126.9 11.9 %collective-permute-start.13 = (bf16[128,1536]{1,0:T(8,128)(2,1)S(1)}, bf16[128,1536]{1,0:T(8,128)(2,1)S(1)}, u32[]{:S(2)}, u32[]{:S(2)}) collective-permute-start(bf16[128,1536]{1,0:T(8,128)(2,1)S(1)} %slice.131), channel_id=1, source_target_pairs={{0,128},{64,192},{128,0},{192,64},{1,129},{65,193},{129,1},{193,65... | collective-permute-start | bytes 1179656 | tf_op jit(solution)/shard_map/pre1_yhi/ppermute | solution.py:42
  140.1 10.9 %collective-permute-start.14 = (bf16[128,1536]{1,0:T(8,128)(2,1)S(1)}, bf16[128,1536]{1,0:T(8,128)(2,1)S(1)}, u32[]{:S(2)}, u32[]{:S(2)}) collective-permute-start(bf16[128,1536]{1,0:T(8,128)(2,1)S(1)} %get-tuple-element.19), channel_id=1, source_target_pairs={{0,128},{64,192},{128,0},{192,64},{1,129},{65,193},{129,1},{193,65... | collective-permute-start | bytes 1179656 | tf_op jit(solution)/shard_map/dh1_yhi/ppermute | solution.py:42
  151.1 4.1 %collective-permute-start.15 = (bf16[256,1536]{1,0:T(8,128)(2,1)S(1)}, bf16[256,1536]{1,0:T(8,128)(2,1)S(1)}, u32[]{:S(2)}, u32[]{:S(2)}) collective-permute-start(bf16[256,1536]{1,0:T(8,128)(2,1)S(1)} %pad_maximum_fusion.5), channel_id=1, source_target_pairs={{0,64},{64,0},{128,192},{192,128},{1,65},{65,1},{129,193},{193,129... | collective-permute-start | bytes 2359304 | tf_op jit(solution)/shard_map/dh1_core/ppermute | solution.py:42
  156.7 18.7 %collective-permute-start.21 = (bf16[96,1024]{1,0:T(8,128)(2,1)}, bf16[96,1024]{1,0:T(8,128)(2,1)}, u32[]{:S(2)}, u32[]{:S(2)}) collective-permute-start(bf16[96,1024]{1,0:T(8,128)(2,1)} %get-tuple-element.55), channel_id=1, source_target_pairs={{0,1},{1,2},{2,3},{3,4},{4,5},{5,6},{6,7},{7,0},{8,9},{9,10},{10,1... | collective-permute-start | bytes 589832 | tf_op jit(solution)/shard_map/sum1_u1/ppermute | solution.py:42
  156.7 18.7 %collective-permute-start.22 = (bf16[96,1024]{1,0:T(8,128)(2,1)}, bf16[96,1024]{1,0:T(8,128)(2,1)}, u32[]{:S(2)}, u32[]{:S(2)}) collective-permute-start(bf16[96,1024]{1,0:T(8,128)(2,1)} %get-tuple-element.56), channel_id=1, source_target_pairs={{0,7},{1,0},{2,1},{3,2},{4,3},{5,4},{6,5},{7,6},{8,15},{9,8},{10,9... | collective-permute-start | bytes 589832 | tf_op jit(solution)/shard_map/sum1_d1/ppermute | solution.py:42
  164.8 12.1 %collective-permute-start.16 = (bf16[64,1536]{1,0:T(8,128)(2,1)}, bf16[64,1536]{1,0:T(8,128)(2,1)}, u32[]{:S(2)}, u32[]{:S(2)}) collective-permute-start(bf16[64,1536]{1,0:T(8,128)(2,1)} %get-tuple-element.39), channel_id=1, source_target_pairs={{0,8},{8,16},{16,24},{24,0},{32,40},{40,48},{48,56},{56,32},{1,9},... | collective-permute-start | bytes 589832 | tf_op jit(solution)/shard_map/g_r1/ppermute | solution.py:42
  166.0 11.0 %collective-permute-start.18 = (bf16[64,1536]{1,0:T(8,128)(2,1)}, bf16[64,1536]{1,0:T(8,128)(2,1)}, u32[]{:S(2)}, u32[]{:S(2)}) collective-permute-start(bf16[64,1536]{1,0:T(8,128)(2,1)} %get-tuple-element.40), channel_id=1, source_target_pairs={{0,24},{8,0},{16,8},{24,16},{32,56},{40,32},{48,40},{56,48},{1,25}... | collective-permute-start | bytes 589832 | tf_op jit(solution)/shard_map/g_l1/ppermute | solution.py:42
  178.9 16.3 %collective-permute-start.19 = (bf16[2,64,1536]{2,1,0:T(8,128)(2,1)}, bf16[2,64,1536]{2,1,0:T(8,128)(2,1)}, u32[]{:S(2)}, u32[]{:S(2)}) collective-permute-start(bf16[2,64,1536]{2,1,0:T(8,128)(2,1)} %pad_maximum_fusion.7), channel_id=1, source_target_pairs={{0,24},{8,0},{16,8},{24,16},{32,56},{40,32},{48,40},{56,48},{1,25}... | collective-permute-start | bytes 1179656 | tf_op jit(solution)/shard_map/g_l2/ppermute | solution.py:42
  180.1 10.1 %collective-permute-start.23 = (bf16[192,1024]{1,0:T(8,128)(2,1)S(1)}, bf16[192,1024]{1,0:T(8,128)(2,1)S(1)}, u32[]{:S(2)}, u32[]{:S(2)}) collective-permute-start(bf16[192,1024]{1,0:T(8,128)(2,1)S(1)} %get-tuple-element.22), channel_id=1, source_target_pairs={{0,1},{1,2},{2,3},{3,4},{4,5},{5,6},{6,7},{7,0},{8,9},{9,10},{10,1... | collective-permute-start | bytes 1179656 | tf_op jit(solution)/shard_map/sum1_u2/ppermute | solution.py:42
  180.1 10.1 %collective-permute-start.24 = (bf16[192,1024]{1,0:T(8,128)(2,1)S(1)}, bf16[192,1024]{1,0:T(8,128)(2,1)S(1)}, u32[]{:S(2)}, u32[]{:S(2)}) collective-permute-start(bf16[192,1024]{1,0:T(8,128)(2,1)S(1)} %get-tuple-element.23), channel_id=1, source_target_pairs={{0,7},{1,0},{2,1},{3,2},{4,3},{5,4},{6,5},{7,6},{8,15},{9,8},{10,9... | collective-permute-start | bytes 1179656 | tf_op jit(solution)/shard_map/sum1_d2/ppermute | solution.py:42
  183.6 11.7 %collective-permute-start.17 = (bf16[2,64,1536]{2,1,0:T(8,128)(2,1)}, bf16[2,64,1536]{2,1,0:T(8,128)(2,1)}, u32[]{:S(2)}, u32[]{:S(2)}) collective-permute-start(bf16[2,64,1536]{2,1,0:T(8,128)(2,1)} %pad_maximum_fusion.6), channel_id=1, source_target_pairs={{0,8},{8,16},{16,24},{24,0},{32,40},{40,48},{48,56},{56,32},{1,9},... | collective-permute-start | bytes 1179656 | tf_op jit(solution)/shard_map/g_r2/ppermute | solution.py:42
  192.6 9.3 %collective-permute-start.25 = (bf16[192,1024]{1,0:T(8,128)(2,1)}, bf16[192,1024]{1,0:T(8,128)(2,1)S(1)}, u32[]{:S(2)}, u32[]{:S(2)}) collective-permute-start(bf16[192,1024]{1,0:T(8,128)(2,1)} %get-tuple-element.25), channel_id=1, source_target_pairs={{0,1},{1,2},{2,3},{3,4},{4,5},{5,6},{6,7},{7,0},{8,9},{9,10},{10,1... | collective-permute-start | bytes 1179656 | tf_op jit(solution)/shard_map/sum1_u3/ppermute | solution.py:42
  192.6 10.8 %collective-permute-start.26 = (bf16[192,1024]{1,0:T(8,128)(2,1)S(1)}, bf16[192,1024]{1,0:T(8,128)(2,1)S(1)}, u32[]{:S(2)}, u32[]{:S(2)}) collective-permute-start(bf16[192,1024]{1,0:T(8,128)(2,1)S(1)} %get-tuple-element.26), channel_id=1, source_target_pairs={{0,7},{1,0},{2,1},{3,2},{4,3},{5,4},{6,5},{7,6},{8,15},{9,8},{10,9... | collective-permute-start | bytes 1179656 | tf_op jit(solution)/shard_map/sum1_d3/ppermute | solution.py:42
  196.4 12.2 %collective-permute-start.20 = (bf16[64,1536]{1,0:T(8,128)(2,1)S(1)}, bf16[64,1536]{1,0:T(8,128)(2,1)S(1)}, u32[]{:S(2)}, u32[]{:S(2)}) collective-permute-start(bf16[64,1536]{1,0:T(8,128)(2,1)S(1)} %fusion.27), channel_id=1, source_target_pairs={{0,32},{8,40},{16,48},{24,56},{32,0},{40,8},{48,16},{56,24},{1,33}... | collective-permute-start | bytes 589832 | tf_op jit(solution)/shard_map/g_ylo/ppermute | solution.py:42
  205.0 15.8 %collective-permute-start.28 = (bf16[192,1024]{1,0:T(8,128)(2,1)S(1)}, bf16[192,1024]{1,0:T(8,128)(2,1)S(1)}, u32[]{:S(2)}, u32[]{:S(2)}) collective-permute-start(bf16[192,1024]{1,0:T(8,128)(2,1)S(1)} %get-tuple-element.28), channel_id=1, source_target_pairs={{0,7},{1,0},{2,1},{3,2},{4,3},{5,4},{6,5},{7,6},{8,15},{9,8},{10,9... | collective-permute-start | bytes 1179656 | tf_op jit(solution)/shard_map/sum1_d4/ppermute | solution.py:42
  208.5 14.1 %collective-permute-start.27 = (bf16[192,1024]{1,0:T(8,128)(2,1)S(1)}, bf16[192,1024]{1,0:T(8,128)(2,1)S(1)}, u32[]{:S(2)}, u32[]{:S(2)}) collective-permute-start(bf16[192,1024]{1,0:T(8,128)(2,1)S(1)} %get-tuple-element.27), channel_id=1, source_target_pairs={{0,1},{1,2},{2,3},{3,4},{4,5},{5,6},{6,7},{7,0},{8,9},{9,10},{10,1... | collective-permute-start | bytes 1179656 | tf_op jit(solution)/shard_map/sum1_u4/ppermute | solution.py:42
  (12 other events, 53.3 us)
Sparse Core Ops, SparseCore 0:
  9.8 40.6 all-gather.2
  52.9 65.1 all-gather.4
  120.6 63.1 reduce-scatter.2
  186.2 41.7 reduce-scatter.4
where the time goes:
time: 239 us; the launch traced here: 237 us
  waiting for transfers between devices  97.7 us (41%)
  starting transfers between devices  53.1 us (22%)
  matrix products  32.3 us (14%)
  local copies, waits for them, and re-layouts  19.9 us (8%)
  other arithmetic  19.8 us (8%)
  between operations  14.1 us (6%)
    ppermute x29, waiting for transfers between devices, send(): return lax.ppermute(value, axis, pairs)  90.5 us
    ppermute x29, starting transfers between devices, send(): return lax.ppermute(value, axis, pairs)  52.9 us
    dot_general x6, matrix products, mm(): return jnp.dot(a, b, preferred_element_type=jnp.float32)  20.6 us
    dot_general x2, matrix products, back(): lax.dot_general(dh, w, (((1,), (1,)), ((), ())), preferred_element_type=j...  11.6 us
  transfers between devices with their start and end apart: 33, of which 19 were waited for; matrix products, arithmetic and copies ran while one was open for 29% of the time, Pallas kernels for 0%

commit v1 on v0

--- a/solution.py
+++ b/solution.py
@@ -148,15 +148,18 @@
     def beside(far):
         g = gi + back(tie(dh1, far), w1)
         p2 = mm(xt, tie(dh1[:, ring:], far)).astype(bf16)
-        return (g,), (p2, gw0), ()
+        return (g, p2), (gw0,), ()
 
-    gw1, ((g,), (p2, _), _) = sum_z(dh1[:, :ring], "sum1", beside)
+    gw1, ((g, p2), _, _) = sum_z(dh1[:, :ring], "sum1", beside)
     gw2 = lax.psum_scatter(p2, "depth", scatter_dimension=0, tiled=True)
     g = sum_out(g)
+    grad_weight = jnp.zeros(weight.shape, bf16)
+    for value, start in ((gw0, 0), (gw2, WIDTHS[0] + ring), (gw1, WIDTHS[0])):
+        grad_weight = lax.dynamic_update_slice(grad_weight, value, (0, start))
     return (
         jnp.concatenate([act0, act1], axis=1),
         g.astype(bf16),
-        jnp.concatenate([gw0, gw1, gw2], axis=1),
+        grad_weight,
     )
 
 

time: 239 us -> 241 us (level)
    reduce_scatter x1, waiting for transfers between devices: 4.07 us -> 16.7 us  [body(): gw2 = lax.psum_scatter(p2, 'depth', scatter_dimension=0, tiled=True)]
    ppermute x29, waiting for transfers between devices: 90.5 us -> 78.1 us  [send(): return lax.ppermute(value, axis, pairs)]
  transfers between devices with their start and end apart: 33 -> 33, of which waited for: 19 -> 17; matrix products, arithmetic and copies ran while one was open for 29% -> 29% of each run, Pallas kernels for 0% -> 0%
where the time goes in v1:
time: 241 us; the launch traced here: 238 us
  waiting for transfers between devices  97.7 us (41%)
  starting transfers between devices  53 us (22%)
  matrix products  32.4 us (13%)
  local copies, waits for them, and re-layouts  22.1 us (9%)
  other arithmetic  18.4 us (8%)
  between operations  14.2 us (6%)
    ppermute x29, waiting for transfers between devices, send(): return lax.ppermute(value, axis, pairs)  78.1 us
    ppermute x29, starting transfers between devices, send(): return lax.ppermute(value, axis, pairs)  52.9 us
    dot_general x6, matrix products, mm(): return jnp.dot(a, b, preferred_element_type=jnp.float32)  20.7 us
    reduce_scatter x1, waiting for transfers between devices, body(): gw2 = lax.psum_scatter(p2, 'depth', scatter_dimension=0, tiled=True)  16.7 us
    dot_general x2, matrix products, back(): lax.dot_general(dh, w, (((1,), (1,)), ((), ())), preferred_element_type=j...  11.7 us
    convert_element_type x2, other arithmetic, sum_z(): u, d = (u.astype(bf16), d.astype(bf16))  4.93 us
  transfers between devices with their start and end apart: 33, of which 17 were waited for; matrix products, arithmetic and copies ran while one was open for 29% of the time, Pallas kernels for 0%

profile of v1, /device:TPU:1, one launch (start us, length us, event | category | flops | bytes accessed | tf_op | source)
XLA Modules:
  0.0 237.8 jit_solution(2748577373764256614)
XLA Ops:
  12.6 3.9 %collective-permute-start.1 = (bf16[192,1536]{1,0:T(8,128)(2,1)S(1)}, bf16[192,1536]{1,0:T(8,128)(2,1)S(1)}, u32[]{:S(2)}, u32[]{:S(2)}) collective-permute-start(bf16[192,1536]{1,0:T(8,128)(2,1)S(1)} %get-tuple-element.54), channel_id=1, source_target_pairs={{0,7},{1,0},{2,1},{3,2},{4,3},{5,4},{6,5},{7,6},{8,15},{9,8},{10,9... | collective-permute-start | bytes 1769480 | tf_op jit(solution)/shard_map/gather_d1/ppermute | solution.py:42
  16.6 2.5 %broadcast_in_dim.32 = bf16[8,192,1536]{2,1,0:T(8,128)(2,1)} broadcast(bf16[]{:T(256)} %constant.306.clone.1), dimensions={} | broadcast | bytes 4718594 | tf_op jit(solution)/shard_map/broadcast_in_dim | solution.py:79
  20.0 9.8 %collective-permute-done = bf16[192,1536]{1,0:T(8,128)(2,1)S(1)} collective-permute-done((bf16[192,1536]{1,0:T(8,128)(2,1)S(1)}, bf16[192,1536]{1,0:T(8,128)(2,1)S(1)}, u32[]{:S(2)}, u32[]{:S(2)}) %collective-permute-start) | collective-permute-done | bytes 589856 | tf_op jit(solution)/shard_map/gather_u1/ppermute | solution.py:42
  29.7 2.7 %collective-permute-start.3 = (bf16[192,1536]{1,0:T(8,128)(2,1)S(1)}, bf16[192,1536]{1,0:T(8,128)(2,1)S(1)}, u32[]{:S(2)}, u32[]{:S(2)}) collective-permute-start(bf16[192,1536]{1,0:T(8,128)(2,1)S(1)} %collective-permute-done.1), channel_id=1, source_target_pairs={{0,7},{1,0},{2,1},{3,2},{4,3},{5,4},{6,5},{7,6},{8,15},{9,8},{10,9... | collective-permute-start | bytes 1769480 | tf_op jit(solution)/shard_map/gather_d2/ppermute | solution.py:42
  34.2 10.5 %collective-permute-done.2 = bf16[192,1536]{1,0:T(8,128)(2,1)S(1)} collective-permute-done((bf16[192,1536]{1,0:T(8,128)(2,1)S(1)}, bf16[192,1536]{1,0:T(8,128)(2,1)S(1)}, u32[]{:S(2)}, u32[]{:S(2)}) %collective-permute-start.2) | collective-permute-done | bytes 589856 | tf_op jit(solution)/shard_map/gather_u2/ppermute | solution.py:42
  44.8 2.7 %collective-permute-start.5 = (bf16[192,1536]{1,0:T(8,128)(2,1)S(1)}, bf16[192,1536]{1,0:T(8,128)(2,1)S(1)}, u32[]{:S(2)}, u32[]{:S(2)}) collective-permute-start(bf16[192,1536]{1,0:T(8,128)(2,1)S(1)} %collective-permute-done.3), channel_id=1, source_target_pairs={{0,7},{1,0},{2,1},{3,2},{4,3},{5,4},{6,5},{7,6},{8,15},{9,8},{10,9... | collective-permute-start | bytes 1769480 | tf_op jit(solution)/shard_map/gather_d3/ppermute | solution.py:42
  49.2 9.5 %collective-permute-done.4 = bf16[192,1536]{1,0:T(8,128)(2,1)S(1)} collective-permute-done((bf16[192,1536]{1,0:T(8,128)(2,1)S(1)}, bf16[192,1536]{1,0:T(8,128)(2,1)S(1)}, u32[]{:S(2)}, u32[]{:S(2)}) %collective-permute-start.4) | collective-permute-done | bytes 589856 | tf_op jit(solution)/shard_map/gather_u3/ppermute | solution.py:42
  58.9 2.7 %collective-permute-start.7 = (bf16[96,1536]{1,0:T(8,128)(2,1)S(1)}, bf16[96,1536]{1,0:T(8,128)(2,1)S(1)}, u32[]{:S(2)}, u32[]{:S(2)}) collective-permute-start(bf16[96,1536]{1,0:T(8,128)(2,1)S(1)} %slice.91), channel_id=1, source_target_pairs={{0,7},{1,0},{2,1},{3,2},{4,3},{5,4},{6,5},{7,6},{8,15},{9,8},{10,9... | collective-permute-start | bytes 884744 | tf_op jit(solution)/shard_map/gather_d4/ppermute | solution.py:42
  69.5 4.6 %fusion.38 = f32[512,1536]{1,0:T(8,128)S(1)} fusion(bf16[1536,1536]{1,0:T(8,128)(2,1)} %bitcast.9, bf16[128,1536]{0,1:T(8,128)(2,1)S(1)} %copy.14, bf16[128,1536]{0,1:T(8,128)(2,1)S(1)} %copy.13, bf16[128,1536]{0,1:T(8,128)(2,1)S(1)} %copy.12, bf16[128,1536]{0,1:T(8,128)(2,1)S(1)} %copy.11), kind=kOutput, calls=%fused_computation.97 | convolution fusion | flops 2422210560 | bytes 9437184 | tf_op jit(solution)/shard_map/dot_general | solution.py:24
  74.3 4.1 %collective-permute-start.8 = (f32[256,1536]{1,0:T(8,128)S(1)}, f32[256,1536]{1,0:T(8,128)S(1)}, u32[]{:S(2)}, u32[]{:S(2)}) collective-permute-start(f32[256,1536]{1,0:T(8,128)S(1)} %slice.93), channel_id=1, source_target_pairs={{0,64},{64,0},{128,192},{192,128},{1,65},{65,1},{129,193},{193,129... | collective-permute-start | bytes 4718600 | tf_op jit(solution)/shard_map/pre0_core/ppermute | solution.py:42
  78.5 3.0 %collective-permute-done.8 = f32[256,1536]{1,0:T(8,128)S(1)} collective-permute-done((f32[256,1536]{1,0:T(8,128)S(1)}, f32[256,1536]{1,0:T(8,128)S(1)}, u32[]{:S(2)}, u32[]{:S(2)}) %collective-permute-start.8) | collective-permute-done | bytes 1572896 | tf_op jit(solution)/shard_map/pre0_core/ppermute | solution.py:42
  81.8 3.1 %collective-permute-start.9 = (bf16[128,1536]{1,0:T(8,128)(2,1)S(1)}, bf16[128,1536]{1,0:T(8,128)(2,1)S(1)}, u32[]{:S(2)}, u32[]{:S(2)}) collective-permute-start(bf16[128,1536]{1,0:T(8,128)(2,1)S(1)} %slice.132), channel_id=1, source_target_pairs={{0,128},{64,192},{128,0},{192,64},{1,129},{65,193},{129,1},{193,65... | collective-permute-start | bytes 1179656 | tf_op jit(solution)/shard_map/pre0_yhi/ppermute | solution.py:42
  84.9 8.9 %collective-permute-done.9 = bf16[128,1536]{1,0:T(8,128)(2,1)S(1)} collective-permute-done((bf16[128,1536]{1,0:T(8,128)(2,1)S(1)}, bf16[128,1536]{1,0:T(8,128)(2,1)S(1)}, u32[]{:S(2)}, u32[]{:S(2)}) %collective-permute-start.9) | collective-permute-done | bytes 393248 | tf_op jit(solution)/shard_map/pre0_yhi/ppermute | solution.py:42
  94.5 3.1 %collective-permute-start.10 = (bf16[128,1536]{1,0:T(8,128)(2,1)S(1)}, bf16[128,1536]{1,0:T(8,128)(2,1)S(1)}, u32[]{:S(2)}, u32[]{:S(2)}) collective-permute-start(bf16[128,1536]{1,0:T(8,128)(2,1)S(1)} %get-tuple-element.46), channel_id=1, source_target_pairs={{0,128},{64,192},{128,0},{192,64},{1,129},{65,193},{129,1},{193,65... | collective-permute-start | bytes 1179656 | tf_op jit(solution)/shard_map/dh0_yhi/ppermute | solution.py:42
  97.6 8.1 %collective-permute-done.10 = bf16[128,1536]{1,0:T(8,128)(2,1)S(1)} collective-permute-done((bf16[128,1536]{1,0:T(8,128)(2,1)S(1)}, bf16[128,1536]{1,0:T(8,128)(2,1)S(1)}, u32[]{:S(2)}, u32[]{:S(2)}) %collective-permute-start.10) | collective-permute-done | bytes 393248 | tf_op jit(solution)/shard_map/dh0_yhi/ppermute | solution.py:42
  111.4 4.4 %convolution_convert_fusion = bf16[1536,1536]{1,0:T(8,128)(2,1)} fusion(bf16[1536,512]{1,0:T(8,128)(2,1)S(1)} %get-tuple-element.47, bf16[256,1536]{1,0:T(8,128)(2,1)S(1)} %collective-permute-done.11, bf16[128,1536]{1,0:T(8,128)(2,1)S(1)} %collective-permute-done.10, bf16[128,1536]{1,0:T(8,128)(2,1)S(1)} %get-tuple-element.46), kind=kOutput, calls=%fused_computation | convolution fusion | flops 2422996992 | bytes 7864320 | tf_op jit(solution)/shard_map/dot_general | solution.py:24
  118.1 4.6 %fusion.41 = f32[512,1536]{1,0:T(8,128)S(1)} fusion(bf16[512,1536]{0,1:T(8,128)(2,1)S(1)} %copy-done.4, bf16[1536,1536]{1,0:T(8,128)(2,1)} %all-gather.5.cloned.1.call-done), kind=kOutput, calls=%fused_computation.100 | convolution fusion | flops 2415919104 | bytes 9437184 | tf_op jit(solution)/shard_map/dot_general | solution.py:24
  123.9 2.7 %collective-permute-done.12 = f32[256,1536]{1,0:T(8,128)S(1)} collective-permute-done((f32[256,1536]{1,0:T(8,128)S(1)}, f32[256,1536]{1,0:T(8,128)S(1)}, u32[]{:S(2)}, u32[]{:S(2)}) %collective-permute-start.12) | collective-permute-done | bytes 1572896 | tf_op jit(solution)/shard_map/pre1_core/ppermute | solution.py:42
  126.9 2.8 %collective-permute-start.13 = (bf16[128,1536]{1,0:T(8,128)(2,1)S(1)}, bf16[128,1536]{1,0:T(8,128)(2,1)S(1)}, u32[]{:S(2)}, u32[]{:S(2)}) collective-permute-start(bf16[128,1536]{1,0:T(8,128)(2,1)S(1)} %slice.131), channel_id=1, source_target_pairs={{0,128},{64,192},{128,0},{192,64},{1,129},{65,193},{129,1},{193,65... | collective-permute-start | bytes 1179656 | tf_op jit(solution)/shard_map/pre1_yhi/ppermute | solution.py:42
  129.7 7.1 %fusion.42 = f32[512,1536]{1,0:T(8,128)} fusion(bf16[512,1536]{1,0:T(8,128)(2,1)S(1)} %pad_maximum_fusion.1, bf16[1536,1536]{1,0:T(8,128)(2,1)} %bitcast.9), kind=kOutput, calls=%fused_computation.101 | convolution fusion | flops 2415919104 | bytes 9437184 | tf_op jit(solution)/shard_map/dot_general | solution.py:105
  140.1 2.8 %collective-permute-start.14 = (bf16[128,1536]{1,0:T(8,128)(2,1)S(1)}, bf16[128,1536]{1,0:T(8,128)(2,1)S(1)}, u32[]{:S(2)}, u32[]{:S(2)}) collective-permute-start(bf16[128,1536]{1,0:T(8,128)(2,1)S(1)} %get-tuple-element.19), channel_id=1, source_target_pairs={{0,128},{64,192},{128,0},{192,64},{1,129},{65,193},{129,1},{193,65... | collective-permute-start | bytes 1179656 | tf_op jit(solution)/shard_map/dh1_yhi/ppermute | solution.py:42
  143.0 8.1 %collective-permute-done.14 = bf16[128,1536]{1,0:T(8,128)(2,1)S(1)} collective-permute-done((bf16[128,1536]{1,0:T(8,128)(2,1)S(1)}, bf16[128,1536]{1,0:T(8,128)(2,1)S(1)}, u32[]{:S(2)}, u32[]{:S(2)}) %collective-permute-start.14) | collective-permute-done | bytes 393248 | tf_op jit(solution)/shard_map/dh1_yhi/ppermute | solution.py:42
  156.7 2.7 %collective-permute-start.22 = (bf16[96,1024]{1,0:T(8,128)(2,1)}, bf16[96,1024]{1,0:T(8,128)(2,1)}, u32[]{:S(2)}, u32[]{:S(2)}) collective-permute-start(bf16[96,1024]{1,0:T(8,128)(2,1)} %get-tuple-element.56), channel_id=1, source_target_pairs={{0,7},{1,0},{2,1},{3,2},{4,3},{5,4},{6,5},{7,6},{8,15},{9,8},{10,9... | collective-permute-start | bytes 589832 | tf_op jit(solution)/shard_map/sum1_d1/ppermute | solution.py:42
  159.3 4.5 %convolution_add_fusion = f32[512,1536]{1,0:T(8,128)S(1)} fusion(f32[512,1536]{1,0:T(8,128)S(1)} %copy-done.12, bf16[512,1536]{1,0:T(8,128)(2,1)S(1)} %constant_dynamic-update-slice_fusion.1, bf16[1536,1536]{1,0:T(8,128)(2,1)} %all-gather.5.cloned.1.call-done), kind=kOutput, calls=%fused_computation.1 | convolution fusion | flops 2416705536 | bytes 12582912 | tf_op jit(solution)/shard_map/dot_general | solution.py:105
  167.5 4.5 %fusion.43 = f32[1536,1024]{1,0:T(8,128)} fusion(bf16[1536,512]{1,0:T(8,128)(2,1)S(1)} %copy-done.3, bf16[512,1024]{1,0:T(8,128)(2,1)S(1)} %slice.100), kind=kOutput, calls=%fused_computation.102 | convolution fusion | flops 1610612736 | bytes 8912896 | tf_op jit(solution)/shard_map/dot_general | solution.py:24
  180.1 2.7 %collective-permute-start.24 = (bf16[192,1024]{1,0:T(8,128)(2,1)S(1)}, bf16[192,1024]{1,0:T(8,128)(2,1)S(1)}, u32[]{:S(2)}, u32[]{:S(2)}) collective-permute-start(bf16[192,1024]{1,0:T(8,128)(2,1)S(1)} %get-tuple-element.24), channel_id=1, source_target_pairs={{0,7},{1,0},{2,1},{3,2},{4,3},{5,4},{6,5},{7,6},{8,15},{9,8},{10,9... | collective-permute-start | bytes 1179656 | tf_op jit(solution)/shard_map/sum1_d2/ppermute | solution.py:42
  184.8 5.3 %collective-permute-done.23 = bf16[192,1024]{1,0:T(8,128)(2,1)S(1)} collective-permute-done((bf16[192,1024]{1,0:T(8,128)(2,1)S(1)}, bf16[192,1024]{1,0:T(8,128)(2,1)S(1)}, u32[]{:S(2)}, u32[]{:S(2)}) %collective-permute-start.23) | collective-permute-done | bytes 393248 | tf_op jit(solution)/shard_map/sum1_u2/ppermute | solution.py:42
  192.5 2.7 %collective-permute-start.26 = (bf16[192,1024]{1,0:T(8,128)(2,1)S(1)}, bf16[192,1024]{1,0:T(8,128)(2,1)S(1)}, u32[]{:S(2)}, u32[]{:S(2)}) collective-permute-start(bf16[192,1024]{1,0:T(8,128)(2,1)S(1)} %get-tuple-element.26), channel_id=1, source_target_pairs={{0,7},{1,0},{2,1},{3,2},{4,3},{5,4},{6,5},{7,6},{8,15},{9,8},{10,9... | collective-permute-start | bytes 1179656 | tf_op jit(solution)/shard_map/sum1_d3/ppermute | solution.py:42
  197.6 4.2 %collective-permute-done.25 = bf16[192,1024]{1,0:T(8,128)(2,1)S(1)} collective-permute-done((bf16[192,1024]{1,0:T(8,128)(2,1)}, bf16[192,1024]{1,0:T(8,128)(2,1)S(1)}, u32[]{:S(2)}, u32[]{:S(2)}) %collective-permute-start.25) | collective-permute-done | bytes 393248 | tf_op jit(solution)/shard_map/sum1_u3/ppermute | solution.py:42
  203.2 2.5 %fusion.17 = (bf16[192,1024]{1,0:T(8,128)(2,1)}, bf16[192,1024]{1,0:T(8,128)(2,1)}) fusion(bf16[192,1024]{1,0:T(8,128)(2,1)S(1)} %collective-permute-done.25, f32[8,192,1024]{2,1,0:T(8,128)} %bitcast.104, s32[]{:T(128)S(6)} %select_n.208, bf16[192,1024]{1,0:T(8,128)(2,1)S(1)} %collective-permute-done.26, s32[]{:T(128)S(6)} %select_n.207), kind=kLoop, calls=%fused_computation.40 | loop fusion | flops 1179648 | bytes 3145736 | tf_op jit(solution)/shard_map/convert_element_type | solution.py:123
  205.7 3.5 %collective-permute-start.28 = (bf16[192,1024]{1,0:T(8,128)(2,1)}, bf16[192,1024]{1,0:T(8,128)(2,1)S(1)}, u32[]{:S(2)}, u32[]{:S(2)}) collective-permute-start(bf16[192,1024]{1,0:T(8,128)(2,1)} %get-tuple-element.28), channel_id=1, source_target_pairs={{0,7},{1,0},{2,1},{3,2},{4,3},{5,4},{6,5},{7,6},{8,15},{9,8},{10,9... | collective-permute-start | bytes 1179656 | tf_op jit(solution)/shard_map/sum1_d4/ppermute | solution.py:42
  211.1 16.7 %reduce-scatter.5.cloned.1.call-done = bf16[192,512]{1,0:T(8,128)(2,1)} async-done(((bf16[1536,512]{1,0:T(8,128)(2,1)}), bf16[192,512]{1,0:T(8,128)(2,1)}) %reduce-scatter.5.cloned.1.call-update) | async-done | bytes 196624 | tf_op jit(solution)/shard_map/reduce_scatter | solution.py:154
  (123 shorter events, 62.6 us)
Async XLA Ops:
  7.2 60.0 %all-gather.3.cloned.1.call-start = ((), (), s32[]{:S(2)}) async-start(), calls=%async_computation.2 | async-start | bytes 1769472 | tf_op jit(solution)/shard_map/all_gather | solution.py:129
  7.9 110.2 %all-gather.5.cloned.1.call-start = ((), (), s32[]{:S(2)}) async-start(), calls=%async_computation.3 | async-start | bytes 5308416 | tf_op jit(solution)/shard_map/all_gather | solution.py:134
  10.2 19.6 %collective-permute-start = (bf16[192,1536]{1,0:T(8,128)(2,1)S(1)}, bf16[192,1536]{1,0:T(8,128)(2,1)S(1)}, u32[]{:S(2)}, u32[]{:S(2)}) collective-permute-start(bf16[192,1536]{1,0:T(8,128)(2,1)S(1)} %get-tuple-element.54), channel_id=1, source_target_pairs={{0,1},{1,2},{2,3},{3,4},{4,5},{5,6},{6,7},{7,0},{8,9},{9,10},{10,1... | collective-permute-start | bytes 1769480 | tf_op jit(solution)/shard_map/gather_u1/ppermute | solution.py:42
  12.6 17.1 %collective-permute-start.1 = (bf16[192,1536]{1,0:T(8,128)(2,1)S(1)}, bf16[192,1536]{1,0:T(8,128)(2,1)S(1)}, u32[]{:S(2)}, u32[]{:S(2)}) collective-permute-start(bf16[192,1536]{1,0:T(8,128)(2,1)S(1)} %get-tuple-element.54), channel_id=1, source_target_pairs={{0,7},{1,0},{2,1},{3,2},{4,3},{5,4},{6,5},{7,6},{8,15},{9,8},{10,9... | collective-permute-start | bytes 1769480 | tf_op jit(solution)/shard_map/gather_d1/ppermute | solution.py:42
  29.7 14.9 %collective-permute-start.2 = (bf16[192,1536]{1,0:T(8,128)(2,1)S(1)}, bf16[192,1536]{1,0:T(8,128)(2,1)S(1)}, u32[]{:S(2)}, u32[]{:S(2)}) collective-permute-start(bf16[192,1536]{1,0:T(8,128)(2,1)S(1)} %collective-permute-done), channel_id=1, source_target_pairs={{0,1},{1,2},{2,3},{3,4},{4,5},{5,6},{6,7},{7,0},{8,9},{9,10},{10,1... | collective-permute-start | bytes 1769480 | tf_op jit(solution)/shard_map/gather_u2/ppermute | solution.py:42
  29.7 15.1 %collective-permute-start.3 = (bf16[192,1536]{1,0:T(8,128)(2,1)S(1)}, bf16[192,1536]{1,0:T(8,128)(2,1)S(1)}, u32[]{:S(2)}, u32[]{:S(2)}) collective-permute-start(bf16[192,1536]{1,0:T(8,128)(2,1)S(1)} %collective-permute-done.1), channel_id=1, source_target_pairs={{0,7},{1,0},{2,1},{3,2},{4,3},{5,4},{6,5},{7,6},{8,15},{9,8},{10,9... | collective-permute-start | bytes 1769480 | tf_op jit(solution)/shard_map/gather_d2/ppermute | solution.py:42
  44.7 147.8 %reduce-scatter.3.cloned.1.call-start = ((), (), s32[]{:S(2)}) async-start(), calls=%async_computation.4 | async-start | bytes 5308416 | tf_op jit(solution)/shard_map/reduce_scatter | solution.py:140
  44.7 14.1 %collective-permute-start.4 = (bf16[192,1536]{1,0:T(8,128)(2,1)S(1)}, bf16[192,1536]{1,0:T(8,128)(2,1)S(1)}, u32[]{:S(2)}, u32[]{:S(2)}) collective-permute-start(bf16[192,1536]{1,0:T(8,128)(2,1)S(1)} %collective-permute-done.2), channel_id=1, source_target_pairs={{0,1},{1,2},{2,3},{3,4},{4,5},{5,6},{6,7},{7,0},{8,9},{9,10},{10,1... | collective-permute-start | bytes 1769480 | tf_op jit(solution)/shard_map/gather_u3/ppermute | solution.py:42
  44.8 14.1 %collective-permute-start.5 = (bf16[192,1536]{1,0:T(8,128)(2,1)S(1)}, bf16[192,1536]{1,0:T(8,128)(2,1)S(1)}, u32[]{:S(2)}, u32[]{:S(2)}) collective-permute-start(bf16[192,1536]{1,0:T(8,128)(2,1)S(1)} %collective-permute-done.3), channel_id=1, source_target_pairs={{0,7},{1,0},{2,1},{3,2},{4,3},{5,4},{6,5},{7,6},{8,15},{9,8},{10,9... | collective-permute-start | bytes 1769480 | tf_op jit(solution)/shard_map/gather_d3/ppermute | solution.py:42
  58.8 6.9 %collective-permute-start.6 = (bf16[96,1536]{1,0:T(8,128)(2,1)S(1)}, bf16[96,1536]{1,0:T(8,128)(2,1)S(1)}, u32[]{:S(2)}, u32[]{:S(2)}) collective-permute-start(bf16[96,1536]{1,0:T(8,128)(2,1)S(1)} %slice.90), channel_id=1, source_target_pairs={{0,1},{1,2},{2,3},{3,4},{4,5},{5,6},{6,7},{7,0},{8,9},{9,10},{10,1... | collective-permute-start | bytes 884744 | tf_op jit(solution)/shard_map/gather_u4/ppermute | solution.py:42
  58.9 7.5 %collective-permute-start.7 = (bf16[96,1536]{1,0:T(8,128)(2,1)S(1)}, bf16[96,1536]{1,0:T(8,128)(2,1)S(1)}, u32[]{:S(2)}, u32[]{:S(2)}) collective-permute-start(bf16[96,1536]{1,0:T(8,128)(2,1)S(1)} %slice.91), channel_id=1, source_target_pairs={{0,7},{1,0},{2,1},{3,2},{4,3},{5,4},{6,5},{7,6},{8,15},{9,8},{10,9... | collective-permute-start | bytes 884744 | tf_op jit(solution)/shard_map/gather_d4/ppermute | solution.py:42
  74.3 7.2 %collective-permute-start.8 = (f32[256,1536]{1,0:T(8,128)S(1)}, f32[256,1536]{1,0:T(8,128)S(1)}, u32[]{:S(2)}, u32[]{:S(2)}) collective-permute-start(f32[256,1536]{1,0:T(8,128)S(1)} %slice.93), channel_id=1, source_target_pairs={{0,64},{64,0},{128,192},{192,128},{1,65},{65,1},{129,193},{193,129... | collective-permute-start | bytes 4718600 | tf_op jit(solution)/shard_map/pre0_core/ppermute | solution.py:42
  81.8 12.0 %collective-permute-start.9 = (bf16[128,1536]{1,0:T(8,128)(2,1)S(1)}, bf16[128,1536]{1,0:T(8,128)(2,1)S(1)}, u32[]{:S(2)}, u32[]{:S(2)}) collective-permute-start(bf16[128,1536]{1,0:T(8,128)(2,1)S(1)} %slice.132), channel_id=1, source_target_pairs={{0,128},{64,192},{128,0},{192,64},{1,129},{65,193},{129,1},{193,65... | collective-permute-start | bytes 1179656 | tf_op jit(solution)/shard_map/pre0_yhi/ppermute | solution.py:42
  94.5 11.1 %collective-permute-start.10 = (bf16[128,1536]{1,0:T(8,128)(2,1)S(1)}, bf16[128,1536]{1,0:T(8,128)(2,1)S(1)}, u32[]{:S(2)}, u32[]{:S(2)}) collective-permute-start(bf16[128,1536]{1,0:T(8,128)(2,1)S(1)} %get-tuple-element.46), channel_id=1, source_target_pairs={{0,128},{64,192},{128,0},{192,64},{1,129},{65,193},{129,1},{193,65... | collective-permute-start | bytes 1179656 | tf_op jit(solution)/shard_map/dh0_yhi/ppermute | solution.py:42
  105.7 4.2 %collective-permute-start.11 = (bf16[256,1536]{1,0:T(8,128)(2,1)S(1)}, bf16[256,1536]{1,0:T(8,128)(2,1)S(1)}, u32[]{:S(2)}, u32[]{:S(2)}) collective-permute-start(bf16[256,1536]{1,0:T(8,128)(2,1)S(1)} %pad_maximum_fusion.2), channel_id=1, source_target_pairs={{0,64},{64,0},{128,192},{192,128},{1,65},{65,1},{129,193},{193,129... | collective-permute-start | bytes 2359304 | tf_op jit(solution)/shard_map/dh0_core/ppermute | solution.py:42
  115.9 112.0 %reduce-scatter.5.cloned.1.call-start = ((), (), s32[]{:S(2)}) async-start(), calls=%async_computation.5 | async-start | bytes 1769472 | tf_op jit(solution)/shard_map/reduce_scatter | solution.py:154
  126.9 11.9 %collective-permute-start.13 = (bf16[128,1536]{1,0:T(8,128)(2,1)S(1)}, bf16[128,1536]{1,0:T(8,128)(2,1)S(1)}, u32[]{:S(2)}, u32[]{:S(2)}) collective-permute-start(bf16[128,1536]{1,0:T(8,128)(2,1)S(1)} %slice.131), channel_id=1, source_target_pairs={{0,128},{64,192},{128,0},{192,64},{1,129},{65,193},{129,1},{193,65... | collective-permute-start | bytes 1179656 | tf_op jit(solution)/shard_map/pre1_yhi/ppermute | solution.py:42
  140.1 10.9 %collective-permute-start.14 = (bf16[128,1536]{1,0:T(8,128)(2,1)S(1)}, bf16[128,1536]{1,0:T(8,128)(2,1)S(1)}, u32[]{:S(2)}, u32[]{:S(2)}) collective-permute-start(bf16[128,1536]{1,0:T(8,128)(2,1)S(1)} %get-tuple-element.19), channel_id=1, source_target_pairs={{0,128},{64,192},{128,0},{192,64},{1,129},{65,193},{129,1},{193,65... | collective-permute-start | bytes 1179656 | tf_op jit(solution)/shard_map/dh1_yhi/ppermute | solution.py:42
  151.1 4.1 %collective-permute-start.15 = (bf16[256,1536]{1,0:T(8,128)(2,1)S(1)}, bf16[256,1536]{1,0:T(8,128)(2,1)S(1)}, u32[]{:S(2)}, u32[]{:S(2)}) collective-permute-start(bf16[256,1536]{1,0:T(8,128)(2,1)S(1)} %pad_maximum_fusion.4), channel_id=1, source_target_pairs={{0,64},{64,0},{128,192},{192,128},{1,65},{65,1},{129,193},{193,129... | collective-permute-start | bytes 2359304 | tf_op jit(solution)/shard_map/dh1_core/ppermute | solution.py:42
  156.7 18.8 %collective-permute-start.21 = (bf16[96,1024]{1,0:T(8,128)(2,1)}, bf16[96,1024]{1,0:T(8,128)(2,1)}, u32[]{:S(2)}, u32[]{:S(2)}) collective-permute-start(bf16[96,1024]{1,0:T(8,128)(2,1)} %get-tuple-element.55), channel_id=1, source_target_pairs={{0,1},{1,2},{2,3},{3,4},{4,5},{5,6},{6,7},{7,0},{8,9},{9,10},{10,1... | collective-permute-start | bytes 589832 | tf_op jit(solution)/shard_map/sum1_u1/ppermute | solution.py:42
  156.7 18.8 %collective-permute-start.22 = (bf16[96,1024]{1,0:T(8,128)(2,1)}, bf16[96,1024]{1,0:T(8,128)(2,1)}, u32[]{:S(2)}, u32[]{:S(2)}) collective-permute-start(bf16[96,1024]{1,0:T(8,128)(2,1)} %get-tuple-element.56), channel_id=1, source_target_pairs={{0,7},{1,0},{2,1},{3,2},{4,3},{5,4},{6,5},{7,6},{8,15},{9,8},{10,9... | collective-permute-start | bytes 589832 | tf_op jit(solution)/shard_map/sum1_d1/ppermute | solution.py:42
  164.8 12.2 %collective-permute-start.16 = (bf16[64,1536]{1,0:T(8,128)(2,1)}, bf16[64,1536]{1,0:T(8,128)(2,1)}, u32[]{:S(2)}, u32[]{:S(2)}) collective-permute-start(bf16[64,1536]{1,0:T(8,128)(2,1)} %get-tuple-element.39), channel_id=1, source_target_pairs={{0,8},{8,16},{16,24},{24,0},{32,40},{40,48},{48,56},{56,32},{1,9},... | collective-permute-start | bytes 589832 | tf_op jit(solution)/shard_map/g_r1/ppermute | solution.py:42
  166.0 11.0 %collective-permute-start.18 = (bf16[64,1536]{1,0:T(8,128)(2,1)}, bf16[64,1536]{1,0:T(8,128)(2,1)}, u32[]{:S(2)}, u32[]{:S(2)}) collective-permute-start(bf16[64,1536]{1,0:T(8,128)(2,1)} %get-tuple-element.40), channel_id=1, source_target_pairs={{0,24},{8,0},{16,8},{24,16},{32,56},{40,32},{48,40},{56,48},{1,25}... | collective-permute-start | bytes 589832 | tf_op jit(solution)/shard_map/g_l1/ppermute | solution.py:42
  178.9 16.3 %collective-permute-start.19 = (bf16[2,64,1536]{2,1,0:T(8,128)(2,1)}, bf16[2,64,1536]{2,1,0:T(8,128)(2,1)}, u32[]{:S(2)}, u32[]{:S(2)}) collective-permute-start(bf16[2,64,1536]{2,1,0:T(8,128)(2,1)} %pad_maximum_fusion.6), channel_id=1, source_target_pairs={{0,24},{8,0},{16,8},{24,16},{32,56},{40,32},{48,40},{56,48},{1,25}... | collective-permute-start | bytes 1179656 | tf_op jit(solution)/shard_map/g_l2/ppermute | solution.py:42
  180.1 10.0 %collective-permute-start.23 = (bf16[192,1024]{1,0:T(8,128)(2,1)S(1)}, bf16[192,1024]{1,0:T(8,128)(2,1)S(1)}, u32[]{:S(2)}, u32[]{:S(2)}) collective-permute-start(bf16[192,1024]{1,0:T(8,128)(2,1)S(1)} %get-tuple-element.23), channel_id=1, source_target_pairs={{0,1},{1,2},{2,3},{3,4},{4,5},{5,6},{6,7},{7,0},{8,9},{9,10},{10,1... | collective-permute-start | bytes 1179656 | tf_op jit(solution)/shard_map/sum1_u2/ppermute | solution.py:42
  180.1 10.0 %collective-permute-start.24 = (bf16[192,1024]{1,0:T(8,128)(2,1)S(1)}, bf16[192,1024]{1,0:T(8,128)(2,1)S(1)}, u32[]{:S(2)}, u32[]{:S(2)}) collective-permute-start(bf16[192,1024]{1,0:T(8,128)(2,1)S(1)} %get-tuple-element.24), channel_id=1, source_target_pairs={{0,7},{1,0},{2,1},{3,2},{4,3},{5,4},{6,5},{7,6},{8,15},{9,8},{10,9... | collective-permute-start | bytes 1179656 | tf_op jit(solution)/shard_map/sum1_d2/ppermute | solution.py:42
  183.5 11.7 %collective-permute-start.17 = (bf16[2,64,1536]{2,1,0:T(8,128)(2,1)}, bf16[2,64,1536]{2,1,0:T(8,128)(2,1)}, u32[]{:S(2)}, u32[]{:S(2)}) collective-permute-start(bf16[2,64,1536]{2,1,0:T(8,128)(2,1)} %pad_maximum_fusion.5), channel_id=1, source_target_pairs={{0,8},{8,16},{16,24},{24,0},{32,40},{40,48},{48,56},{56,32},{1,9},... | collective-permute-start | bytes 1179656 | tf_op jit(solution)/shard_map/g_r2/ppermute | solution.py:42
  192.5 9.3 %collective-permute-start.25 = (bf16[192,1024]{1,0:T(8,128)(2,1)}, bf16[192,1024]{1,0:T(8,128)(2,1)S(1)}, u32[]{:S(2)}, u32[]{:S(2)}) collective-permute-start(bf16[192,1024]{1,0:T(8,128)(2,1)} %get-tuple-element.25), channel_id=1, source_target_pairs={{0,1},{1,2},{2,3},{3,4},{4,5},{5,6},{6,7},{7,0},{8,9},{9,10},{10,1... | collective-permute-start | bytes 1179656 | tf_op jit(solution)/shard_map/sum1_u3/ppermute | solution.py:42
  192.5 10.7 %collective-permute-start.26 = (bf16[192,1024]{1,0:T(8,128)(2,1)S(1)}, bf16[192,1024]{1,0:T(8,128)(2,1)S(1)}, u32[]{:S(2)}, u32[]{:S(2)}) collective-permute-start(bf16[192,1024]{1,0:T(8,128)(2,1)S(1)} %get-tuple-element.26), channel_id=1, source_target_pairs={{0,7},{1,0},{2,1},{3,2},{4,3},{5,4},{6,5},{7,6},{8,15},{9,8},{10,9... | collective-permute-start | bytes 1179656 | tf_op jit(solution)/shard_map/sum1_d3/ppermute | solution.py:42
  196.2 13.0 %collective-permute-start.20 = (bf16[64,1536]{1,0:T(8,128)(2,1)S(1)}, bf16[64,1536]{1,0:T(8,128)(2,1)S(1)}, u32[]{:S(2)}, u32[]{:S(2)}) collective-permute-start(bf16[64,1536]{1,0:T(8,128)(2,1)S(1)} %fusion.28), channel_id=1, source_target_pairs={{0,32},{8,40},{16,48},{24,56},{32,0},{40,8},{48,16},{56,24},{1,33}... | collective-permute-start | bytes 589832 | tf_op jit(solution)/shard_map/g_ylo/ppermute | solution.py:42
  205.7 23.1 %collective-permute-start.28 = (bf16[192,1024]{1,0:T(8,128)(2,1)}, bf16[192,1024]{1,0:T(8,128)(2,1)S(1)}, u32[]{:S(2)}, u32[]{:S(2)}) collective-permute-start(bf16[192,1024]{1,0:T(8,128)(2,1)} %get-tuple-element.28), channel_id=1, source_target_pairs={{0,7},{1,0},{2,1},{3,2},{4,3},{5,4},{6,5},{7,6},{8,15},{9,8},{10,9... | collective-permute-start | bytes 1179656 | tf_op jit(solution)/shard_map/sum1_d4/ppermute | solution.py:42
  209.2 19.6 %collective-permute-start.27 = (bf16[192,1024]{1,0:T(8,128)(2,1)}, bf16[192,1024]{1,0:T(8,128)(2,1)}, u32[]{:S(2)}, u32[]{:S(2)}) collective-permute-start(bf16[192,1024]{1,0:T(8,128)(2,1)} %get-tuple-element.27), channel_id=1, source_target_pairs={{0,1},{1,2},{2,3},{3,4},{4,5},{5,6},{6,7},{7,0},{8,9},{9,10},{10,1... | collective-permute-start | bytes 1179656 | tf_op jit(solution)/shard_map/sum1_u4/ppermute | solution.py:42
  (14 other events, 86.6 us)
Sparse Core Ops, SparseCore 0:
  9.8 40.6 all-gather.2
  52.9 65.1 all-gather.4
  120.6 63.1 reduce-scatter.2
  186.2 41.5 reduce-scatter.4
